TPU v7x, 128 devices: a whole 4x4x4 slice. The times are simulated.
128 devices in a mesh: freq: 32 (over z, x, core), pair: 4 (over y).
Axes of the slice: x: 4, y: 4, z: 4, core: 2. Of those that a mesh axis runs over, the one named last changes fastest.
Arguments:
- voltages: int32 [2048, 103, 2048], P(('pair', 'freq')), may hold values from -8 to 7
- gains: float32 [2048, 96], P(('pair', 'freq')), may hold values from 0.3 to 3
Outputs:
- visibilities: bfloat16 [96, 2, 2048, 2048], P('freq', None, 'pair')
All inputs are finite; a program needn't handle non-finite values.
Results may differ from a plain program's by a relative error of at most 0.0078.
Values may be sent and summed in bfloat16 or wider, within the bound.
A program may use at most 128 MiB of HBM per device.

v0:
```python
import math

import jax
import jax.numpy as jnp
from jax import lax
from jax.sharding import PartitionSpec as P

NFFT = 2048
TAPS = 8
SAMPLES = 96
FIRST = 256


def filter_table():
    positions = jnp.arange(TAPS * NFFT, dtype=jnp.float32)
    span_width = float(TAPS * NFFT)
    window = 0.5 - 0.5 * jnp.cos(2.0 * jnp.pi * (positions + 0.5) / span_width)
    taps_table = window * jnp.sinc((positions - span_width / 2 + 0.5) / NFFT)
    return taps_table.reshape(TAPS, NFFT)


def dft_table(first_bin, count):
    samples = jnp.arange(NFFT, dtype=jnp.int32)
    bin_index = first_bin + jnp.arange(count, dtype=jnp.int32)
    phases = bin_index[:, None] * samples[None, :] % NFFT
    angles = phases.astype(jnp.float32) * (2.0 * math.pi / NFFT)
    amplitude = 0.25 / math.sqrt(NFFT)
    cos_rows = (jnp.cos(angles) * amplitude).astype(jnp.bfloat16)
    sin_rows = (-jnp.sin(angles) * amplitude).astype(jnp.bfloat16)
    return (cos_rows, sin_rows)


def correlate(row_side, col_side):
    row_real, row_imag = (row_side[0], row_side[1])
    col_real, col_imag = (col_side[0], col_side[1])

    def contract(left_side, right_side):
        return jnp.einsum("csr,csk->crk", left_side, right_side, preferred_element_type=jnp.float32)

    real_sum = contract(row_real, col_real) + contract(row_imag, col_imag)
    imag_sum = contract(row_imag, col_real) - contract(row_real, col_imag)
    result = jnp.stack([real_sum, imag_sum], axis=1)
    return (result * (1.0 / SAMPLES)).astype(jnp.bfloat16)


def body(voltages, gains):
    n_freq = lax.axis_size("freq")
    local_inputs = voltages.shape[0]
    all_channels = gains.shape[1]
    ch_dev = all_channels // n_freq
    taps_table = filter_table()
    as_float = voltages.astype(jnp.float32)
    filtered = taps_table[0] * as_float[:, 0:SAMPLES, :]
    for tap_index in range(1, TAPS):
        filtered = (
            filtered + taps_table[tap_index] * as_float[:, tap_index : tap_index + SAMPLES, :]
        )
    filtered = filtered.astype(jnp.bfloat16).reshape(local_inputs * SAMPLES, NFFT)
    cos_rows, sin_rows = dft_table(FIRST, all_channels)
    dft_rows = jnp.stack(
        [cos_rows.reshape(n_freq, ch_dev, NFFT), sin_rows.reshape(n_freq, ch_dev, NFFT)], 1
    )
    dft_rows = dft_rows.reshape(2 * all_channels, NFFT)
    spectra = lax.dot_general(
        dft_rows, filtered, (((1,), (1,)), ((), ())), preferred_element_type=jnp.float32
    )
    gain_rows = jnp.broadcast_to(
        gains.T.reshape(n_freq, 1, ch_dev, local_inputs), (n_freq, 2, ch_dev, local_inputs)
    )
    gain_rows = gain_rows.reshape(2 * all_channels, local_inputs, 1)
    spectra = spectra.reshape(2 * all_channels, local_inputs, SAMPLES) * gain_rows
    spectra = spectra.astype(jnp.bfloat16).reshape(2 * all_channels, local_inputs * SAMPLES)
    turned = lax.all_to_all(spectra, "freq", split_axis=0, concat_axis=1, tiled=True)
    row_side = turned.reshape(2, ch_dev, n_freq * local_inputs, SAMPLES).transpose(0, 1, 3, 2)
    return correlate(row_side, lax.all_gather(row_side, "pair", axis=3, tiled=True))


def solution(mesh):
    placed = (P(("pair", "freq"), None, None), P(("pair", "freq"), None))
    return jax.shard_map(
        body, mesh=mesh, in_specs=placed, out_specs=P("freq", None, "pair", None), check_vma=False
    )
```

profile of v0, /device:TPU:1, one launch (start us, length us, event | category | flops | bytes accessed | tf_op | source)
XLA Modules:
  0.0 170.9 jit_solution(5869198607434618438)
XLA Ops:
  6.5 0.0 all-gather.2.cloned.1.call-start
  6.5 0.3 fusion.25
  6.9 0.8 copy.14
  7.8 0.1 copy.15
  7.8 3.7 %multiply_convert_fusion.2 = (bf16[32,1,3,2048]{3,0,2,1:T(8,128)(2,1)S(1)}, bf16[32,1,3,2048]{3,0,2,1:T(8,128)(2,1)S(1)}) fusion(s32[32,3]{0,1:T(4,128)S(1)} %add_add_fusion), kind=kLoop, calls=%fused_computation.35 | loop fusion | flops 3735552 | bytes 786816 | tf_op jit(solution)/shard_map/convert_element_type | solution.py:28
  11.5 0.1 pad_maximum_fusion
  11.6 0.7 copy.12
  12.3 0.7 reshape.137
  13.0 12.6 %convert_element_type.56 = f32[16,103,2048]{2,0,1:T(8,128)} convert(s32[16,103,2048]{2,0,1:T(8,128)} %param.2) | non-fusion elementwise | flops 3375104 | bytes 27000832 | tf_op jit(solution)/shard_map/convert_element_type | solution.py:52
  25.6 36.5 %fusion.2 = bf16[16,96,2048]{2,0,1:T(8,128)(2,1)} fusion(f32[16,103,2048]{2,0,1:T(8,128)} %convert_element_type.56, f32[2048]{0:T(1024)S(1)} %get-tuple-element.6, f32[2048]{0:T(1024)S(1)} %get-tuple-element.7, f32[2048]{0:T(1024)S(1)} %get-tuple-element.8, f32[2048]{0:T(1024)S(1)} %get-tuple-element.9, f32[2048]{0:T(1024)S(1)} %get-tuple-element.10, ...), kind=kLoop, calls=%fused_computation.4 | loop fusion | flops 50331648 | bytes 107020288 | tf_op jit(solution)/shard_map/convert_element_type | solution.py:58
  62.2 10.4 %multiply_convert_fusion = bf16[192,16,96]{2,0,1:T(8,128)(2,1)S(1)} fusion(bf16[192,2048,1]{1,0,2:T(8,128)(2,1)S(1)} %reshape.137, bf16[16,96,2048]{2,0,1:T(8,128)(2,1)} %fusion.2, f32[192,16]{0,1:T(8,128)S(1)} %copy.15), kind=kOutput, calls=%fused_computation.22 | convolution fusion | flops 1208549376 | bytes 7680000 | tf_op jit(solution)/shard_map/dot_general | solution.py:64
  72.6 0.5 copy.16
  73.1 1.0 all_to_all.12
  74.1 23.5 %all_to_all.16 = bf16[32,6,1536]{2,1,0:T(8,128)(2,1)S(1)} all-to-all(bf16[32,6,1536]{2,1,0:T(8,128)(2,1)S(1)} %all_to_all.12), channel_id=1, replica_groups=mesh['freq'=32,'pair'=4] {'freq'}, dimensions={0} | all-to-all | bytes 1179648 | tf_op jit(solution)/shard_map/all_to_all | solution.py:73
  97.5 0.2 copy.17
  97.7 0.7 reshape.136
  98.4 1.1 copy.18
  99.5 0.0 copy-start.2
  99.5 0.0 all-gather.2.cloned.1.call-update
  99.5 30.9 %all-gather.2.cloned.1.call-done = bf16[2,3,96,2048]{3,2,1,0:T(8,128)(2,1)} async-done(((bf16[2,3,96,512]{3,2,1,0:T(8,128)(2,1)}), bf16[2,3,96,2048]{3,2,1,0:T(8,128)(2,1)}) %all-gather.2.cloned.1.call-update) | async-done | bytes 2359312 | tf_op jit(solution)/shard_map/all_gather | solution.py:75
  130.4 0.0 copy-start.1
  130.4 3.3 %fusion.13 = f32[3,512,2048]{2,1,0:T(8,128)S(1)} fusion(bf16[2,3,96,2048]{3,2,1,0:T(8,128)(2,1)} %all-gather.2.cloned.1.call-done, bf16[2,3,96,512]{3,2,1,0:T(8,128)(2,1)} %bitcast.25), kind=kOutput, calls=%fused_computation.28 | convolution fusion | flops 603979776 | bytes 14057472 | tf_op jit(solution)/shard_map/csr,csk->crk/dot_general | solution.py:38
  133.7 0.0 copy-done.2
  133.7 0.0 copy-done.1
  133.7 1.8 %fusion.14 = f32[3,512,2048]{2,1,0:T(8,128)S(1)} fusion(bf16[2,3,96,2048]{3,2,1,0:T(8,128)(2,1)S(1)} %copy-done.1, bf16[2,3,96,512]{3,2,1,0:T(8,128)(2,1)S(1)} %bitcast.26), kind=kOutput, calls=%fused_computation.29 | convolution fusion | flops 603979776 | bytes 14057472 | tf_op jit(solution)/shard_map/csr,csk->crk/dot_general | solution.py:38
  135.6 7.9 %subtract_bitcast_fusion = f32[3,1,512,2048]{3,2,0,1:T(8,128)} fusion(f32[3,512,2048]{2,1,0:T(8,128)S(1)} %fusion.13, bf16[2,3,96,2048]{3,2,1,0:T(8,128)(2,1)} %all-gather.2.cloned.1.call-done, bf16[2,3,96,512]{3,2,1,0:T(8,128)(2,1)S(1)} %bitcast.27), kind=kOutput, calls=%fused_computation.18 | convolution fusion | flops 607125504 | bytes 26640384 | tf_op jit(solution)/shard_map/csr,csk->crk/dot_general | solution.py:38
  143.4 0.0 copy-start
  143.4 8.2 %add_bitcast_fusion = f32[3,1,512,2048]{3,2,0,1:T(8,128)} fusion(f32[3,512,2048]{2,1,0:T(8,128)S(1)} %fusion.14, bf16[2,3,96,2048]{3,2,1,0:T(8,128)(2,1)} %all-gather.2.cloned.1.call-done, bf16[2,3,96,512]{3,2,1,0:T(8,128)(2,1)S(1)} %bitcast.28), kind=kOutput, calls=%fused_computation.19 | convolution fusion | flops 607125504 | bytes 26640384 | tf_op jit(solution)/shard_map/csr,csk->crk/dot_general | solution.py:38
  151.7 0.0 copy-done
  151.7 7.3 %fusion = bf16[3,2,512,2048]{3,2,0,1:T(8,128)(2,1)S(1)} fusion(f32[3,1,512,2048]{3,2,0,1:T(8,128)S(1)} %copy-done, f32[3,1,512,2048]{3,2,0,1:T(8,128)} %add_bitcast_fusion), kind=kLoop, calls=%fused_computation.1 | loop fusion | flops 18874368 | bytes 37748736 | tf_op jit(solution)/shard_map/convert_element_type | solution.py:43
  159.0 5.1 %copy.19 = bf16[3,2,512,2048]{3,2,1,0:T(8,128)(2,1)} copy(bf16[3,2,512,2048]{3,2,0,1:T(8,128)(2,1)S(1)} %fusion) | data formatting | bytes 25165824 | tf_op jit(solution)/shard_map/convert_element_type | solution.py:43
  (5 shorter events, 0.1 us)
Async XLA Ops:
  6.5 123.8 %all-gather.2.cloned.1.call-start = ((), (), s32[]{:S(2)}) async-start(), calls=%async_computation.1 | async-start | bytes 2949120 | tf_op jit(solution)/shard_map/all_gather | solution.py:75
  99.5 34.2 %copy-start.2 = (bf16[2,3,512,96]{2,3,1,0:T(8,128)(2,1)S(1)}, bf16[2,3,512,96]{2,3,1,0:T(8,128)(2,1)}, u32[]{:S(2)}) copy-start(bf16[2,3,512,96]{2,3,1,0:T(8,128)(2,1)} %copy.18) | copy-start | bytes 1769476
  130.4 3.4 %copy-start.1 = (bf16[2,3,96,2048]{3,2,1,0:T(8,128)(2,1)S(1)}, bf16[2,3,96,2048]{3,2,1,0:T(8,128)(2,1)}, u32[]{:S(2)}) copy-start(bf16[2,3,96,2048]{3,2,1,0:T(8,128)(2,1)} %all-gather.2.cloned.1.call-done) | copy-start | bytes 7077892
  143.4 8.2 %copy-start = (f32[3,1,512,2048]{3,2,0,1:T(8,128)S(1)}, f32[3,1,512,2048]{3,2,0,1:T(8,128)}, u32[]{:S(2)}) copy-start(f32[3,1,512,2048]{3,2,0,1:T(8,128)} %subtract_bitcast_fusion) | copy-start | bytes 37748740
Sparse Core Ops, SparseCore 0:
  99.6 30.6 all-gather.1
where the time goes:
time: 171 us
  other arithmetic  60.6 us (35%)
  matrix products  31.7 us (19%)
  waiting for transfers between devices  30.9 us (18%)
  blocking collectives  23.5 us (14%)
  between operations  13.5 us (8%)
  local copies, waits for them, and re-layouts  10.8 us (6%)
    convert_element_type x1, other arithmetic, body(): filtered.astype(jnp.bfloat16).reshape(local_inputs * SAMPLES, NFFT)  36.5 us
    all_gather x1, waiting for transfers between devices, body(): lax.all_gather(row_side, 'pair', axis=3, tiled=True)  30.9 us
    all_to_all x1, blocking collectives, body(): lax.all_to_all(spectra, 'freq', split_axis=0, concat_axis=1, tiled=True)  23.5 us
    dot_general x4, matrix products, contract(): jnp.einsum('csr,csk->crk', left_side, right_side, preferred_element_type=...  21.3 us
    convert_element_type x1, other arithmetic, body(): as_float = voltages.astype(jnp.float32)  12.6 us
    dot_general x1, matrix products, body(): lax.dot_general(dft_rows, filtered, (((1,), (1,)), ((), ())), preferred_e...  10.4 us
    convert_element_type x1, other arithmetic, correlate(): return (result * (1.0 / SAMPLES)).astype(jnp.bfloat16)  7.3 us
    convert_element_type x1, local copies, waits for them, and re-layouts, correlate(): return (result * (1.0 / SAMPLES)).astype(jnp.bfloat16)  5.08 us
  transfers between devices with their start and end apart: 1, of which 1 were waited for; matrix products, arithmetic and copies ran while one was open for 0% of the time, Pallas kernels for 0%

commit v1 on v0

v1 whole, which is shorter than its diff:
```python
import functools
import math

import jax
import jax.numpy as jnp
import numpy as np
from jax import lax
from jax.experimental import pallas as pl
from jax.experimental.pallas import tpu as pltpu
from jax.sharding import PartitionSpec as P

NFFT = 2048
TAPS = 8
SAMPLES = 96
FRAMES = 103
FIRST = 256
CHANNELS = 96
CHUNKS = 3
SPECTRA = SAMPLES // CHUNKS
INPUTS = 16
LANES = 128
GROUPS = ((0, 0), (0, 1), (1, 0), (1, 1), (2, 0), (2, 1), (2, 0), (2, 1))
SENT = ((0, 1), (1, 2), (3, 2))
VMEM_LIMIT = 56 * 1024 * 1024


def filter_table():
    positions = np.arange(TAPS * NFFT, dtype=np.float64)
    span_width = float(TAPS * NFFT)
    window = 0.5 - 0.5 * np.cos(2.0 * np.pi * (positions + 0.5) / span_width)
    taps_table = window * np.sinc((positions - span_width / 2 + 0.5) / NFFT)
    return taps_table.astype(np.float32).reshape(TAPS, NFFT)


def dft_table():
    samples = np.arange(NFFT)
    bins = FIRST + np.arange(CHANNELS)
    angles = (bins[:, None] * samples[None, :] % NFFT) * (2.0 * math.pi / NFFT)
    amplitude = 0.25 / math.sqrt(NFFT)
    tables = np.stack([np.cos(angles) * amplitude, -np.sin(angles) * amplitude])
    columns = [tables[part, channel::3] for channel, part in GROUPS]
    return np.concatenate(columns, 0).T.astype(np.float32)


def exchange_lanes(rows):
    lane = lax.broadcasted_iota(jnp.int32, rows[0].shape, 1)
    step = len(rows) // 2
    while step:
        odd = (lane & step) != 0
        out = list(rows)
        for s in range(len(rows)):
            if not s & step:
                low, high = rows[s], rows[s + step]
                out[s] = jnp.where(odd, pltpu.roll(high, step, 1), low)
                out[s + step] = jnp.where(odd, high, pltpu.roll(low, LANES - step, 1))
        rows, step = out, step // 2
    return rows


def spectra_kernel(
    n_freq, n_pair, v_hbm, taps_hbm, dft_hbm, gains_ref, g_ref, h_ref,
    v_buf, taps_raw, taps_buf, dft_buf, gain_buf, f0, f1, y_ref, c2_ref, w_ref,
    v_sem, table_sem, turn_send, turn_recv, own_sem, side_send, side_recv, pass_send, pass_recv,
):
    me = lax.axis_index("freq")
    row = lax.axis_index("pair")
    right, left = lax.rem(row + 1, n_pair), lax.rem(row + n_pair - 1, n_pair)

    tables = [
        pltpu.make_async_copy(taps_hbm, taps_raw, table_sem.at[0]),
        pltpu.make_async_copy(dft_hbm, dft_buf, table_sem.at[1]),
    ]
    tables[0].start()
    history = TAPS - 1
    loads = []
    for chunk in range(CHUNKS):
        first = 0 if chunk == 0 else chunk * SPECTRA + history
        frames = pl.ds(first, (chunk + 1) * SPECTRA + history - first)
        loads.append(pltpu.make_async_copy(v_hbm.at[frames], v_buf.at[frames], v_sem.at[chunk]))
        loads[-1].start()
        if chunk == 0:
            tables[1].start()

    barrier = pltpu.get_barrier_semaphore()

    def greet(j, carry):
        pl.semaphore_signal(barrier, inc=1, device_id={"freq": lax.rem(me + j, n_freq)})
        return carry

    lax.fori_loop(1, n_freq, greet, 0)
    for side in (left, right):
        pl.semaphore_signal(barrier, inc=1, device_id={"pair": side})

    lane = lax.broadcasted_iota(jnp.int32, (CHANNELS, 2 * LANES), 1)
    chan = lax.broadcasted_iota(jnp.int32, (CHANNELS, 2 * LANES), 0)
    wanted = 3 * (lane % 32) + jnp.minimum(lane // 64, 2)
    picks = jnp.where(chan == wanted, 1.0, 0.0).astype(jnp.float32)
    gain_buf[...] = jnp.dot(
        gains_ref[...], picks, precision=lax.Precision.HIGHEST, preferred_element_type=jnp.float32
    )
    tables[0].wait()
    for t in range(TAPS):
        for n in range(NFFT // LANES):
            taps_buf[t, n] = jnp.broadcast_to(
                taps_raw[t : t + 1, n * LANES : (n + 1) * LANES], (8, LANES)
            )

    def filter_slice(chunk, q, out):
        for u in range(2):
            n = 2 * q + u
            col = pl.ds(pl.multiple_of(n * LANES, LANES), LANES)
            taps = [taps_buf[t, n] for t in range(TAPS)]

            def frame(s, half):
                return v_buf[chunk * SPECTRA + s, half * 8 : half * 8 + 8, col].astype(jnp.float32)

            window = [[frame(s, half) for s in range(TAPS)] for half in range(2)]
            for s in range(SPECTRA):
                halves = []
                for half in range(2):
                    if s > 0:
                        window[half] = window[half][1:] + [frame(s + TAPS - 1, half)]
                    terms = [taps[t] * window[half][t] for t in range(TAPS)]
                    while len(terms) > 1:
                        terms = [a + b for a, b in zip(terms[::2], terms[1::2])]
                    halves.append(terms[0])
                out[s * INPUTS : (s + 1) * INPUTS, u * LANES : (u + 1) * LANES] = jnp.concatenate(
                    halves, 0
                ).astype(jnp.bfloat16)

    def transform_slice(q, filtered, start=False):
        rows = pl.ds(pl.multiple_of(q * 2 * LANES, 2 * LANES), 2 * LANES)
        part = jnp.dot(filtered[...], dft_buf[rows, :], preferred_element_type=jnp.float32)
        if start:
            y_ref[...] = part
        else:
            y_ref[...] += part

    def channelize(chunk):
        loads[chunk].wait()
        filter_slice(chunk, 0, f0)
        if chunk == 0:
            tables[1].wait()
        transform_slice(0, f0, True)
        filter_slice(chunk, 1, f1)

        def step(j, carry):
            transform_slice(2 * j - 1, f1)
            filter_slice(chunk, 2 * j, f0)
            transform_slice(2 * j, f0)
            filter_slice(chunk, 2 * j + 1, f1)
            return carry

        lax.fori_loop(1, NFFT // LANES // 4, step, 0)
        transform_slice(NFFT // LANES // 2 - 1, f1)

    def rearrange(chunk):
        def spread(rows, tile):
            for f, block in enumerate(exchange_lanes(rows)):
                w_ref[f, tile] = block

        tile = SENT[chunk][0]
        at = [slice(s * INPUTS, (s + 1) * INPUTS) for s in range(SPECTRA)]
        spread([(y_ref[r, :LANES] * gain_buf[:, :LANES]).astype(jnp.bfloat16) for r in at], tile)
        if chunk == 0:
            c2_ref[...] = y_ref[:, LANES:]
            return
        lane = lax.broadcasted_iota(jnp.int32, (INPUTS, LANES), 1)
        rows = []
        for r in at:
            part = y_ref[r, LANES:]
            if chunk == 1:
                part = jnp.where(lane < 64, c2_ref[r, :], part)
            rows.append((part * gain_buf[:, LANES:]).astype(jnp.bfloat16))
        spread(rows, tile + 1)

    def turn(chunk):
        first, tiles = SENT[chunk]

        def send(j, carry):
            f = lax.rem(me + j, n_freq)
            pltpu.make_async_remote_copy(
                src_ref=w_ref.at[f, pl.ds(first, tiles)],
                dst_ref=g_ref.at[row, pl.ds(first, tiles), me],
                send_sem=turn_send.at[chunk],
                recv_sem=turn_recv.at[chunk],
                device_id={"freq": f},
            ).start()
            return carry

        lax.fori_loop(1, n_freq, send, 0)
        pltpu.make_async_copy(
            w_ref.at[me, pl.ds(first, tiles)], g_ref.at[row, pl.ds(first, tiles), me], own_sem.at[chunk]
        ).start()

    def turn_bytes(chunk):
        first, tiles = SENT[chunk]
        block = w_ref.at[pl.ds(0, n_freq - 1), pl.ds(first, tiles)]
        return pltpu.make_async_remote_copy(
            src_ref=block, dst_ref=block, send_sem=turn_send.at[chunk], recv_sem=turn_recv.at[chunk],
            device_id={"freq": me},
        )

    def turned(chunk):
        first, tiles = SENT[chunk]
        turn_bytes(chunk).wait_recv()
        block = w_ref.at[0, pl.ds(first, tiles)]
        pltpu.make_async_copy(block, block, own_sem.at[chunk]).wait()

    def piece(k, block, half):
        if k == 3:
            pairs = n_freq // 2
            return h_ref.at[block] if half is None else h_ref.at[block, pl.ds(half * pairs // 2, pairs // 2)]
        first, tiles = ((0, 1), (1, 2), (3, 1))[k]
        if half is None:
            return g_ref.at[block, pl.ds(first, tiles)]
        return g_ref.at[block, pl.ds(first, tiles), pl.ds(half * n_freq // 2, n_freq // 2)]

    def side_copy(k, to_right):
        ref = piece(k, row, None)
        return pltpu.make_async_remote_copy(
            src_ref=ref, dst_ref=ref, send_sem=side_send.at[k, int(to_right)], recv_sem=side_recv.at[k, int(to_right)],
            device_id={"pair": right if to_right else left},
        )

    def pass_copy(k, to_right):
        ref = piece(k, left if to_right else right, 0 if to_right else 1)
        return pltpu.make_async_remote_copy(
            src_ref=ref, dst_ref=ref, send_sem=pass_send.at[k, int(to_right)], recv_sem=pass_recv.at[k, int(to_right)],
            device_id={"pair": right if to_right else left},
        )

    def spread(k):
        for to_right in (True, False):
            side_copy(k, to_right).start()

    def forward(k):
        for to_right in (True, False):
            side_copy(k, to_right).wait_recv()
            pass_copy(k, to_right).start()

    channelize(0)
    rearrange(0)
    pl.semaphore_wait(barrier, n_freq + 1)
    turn(0)
    channelize(1)
    turned(0)
    spread(0)
    rearrange(1)
    turn(1)
    channelize(2)
    turned(1)
    spread(1)
    forward(0)
    rearrange(2)
    turn(2)
    turned(2)
    spread(2)
    lane = lax.broadcasted_iota(jnp.int32, (INPUTS, LANES), 1)
    for pair in range(n_freq // 2):
        h_ref[row, pair] = jnp.where(lane < 64, g_ref[row, 4, 2 * pair], g_ref[row, 4, 2 * pair + 1])
    spread(3)
    forward(1)
    forward(2)
    forward(3)
    for k in range(4):
        for to_right in (True, False):
            pass_copy(k, to_right).wait_recv()
    for k in range(4):
        for to_right in (True, False):
            side_copy(k, to_right).wait_send()
            pass_copy(k, to_right).wait_send()
    for chunk in range(CHUNKS):
        turn_bytes(chunk).wait_send()


def spectra_call(n_freq, n_pair, voltages, taps_table, dft, gains):
    bf16 = jnp.bfloat16
    anywhere = pl.BlockSpec(memory_space=pl.ANY)
    vmem = pl.BlockSpec(memory_space=pltpu.VMEM)
    dma = pltpu.SemaphoreType.DMA
    return pl.pallas_call(
        functools.partial(spectra_kernel, n_freq, n_pair),
        out_shape=(
            jax.ShapeDtypeStruct((n_pair, 5, n_freq, INPUTS, LANES), bf16),
            jax.ShapeDtypeStruct((n_pair, n_freq // 2, INPUTS, LANES), bf16),
        ),
        in_specs=[anywhere, anywhere, anywhere, vmem],
        out_specs=(vmem, vmem),
        scratch_shapes=[
            pltpu.VMEM((FRAMES, INPUTS, NFFT), jnp.int32),
            pltpu.VMEM((TAPS, NFFT), jnp.float32),
            pltpu.VMEM((TAPS, NFFT // LANES, 8, LANES), jnp.float32),
            pltpu.VMEM((NFFT, 2 * LANES), bf16),
            pltpu.VMEM((INPUTS, 2 * LANES), jnp.float32),
            pltpu.VMEM((SPECTRA * INPUTS, 2 * LANES), bf16),
            pltpu.VMEM((SPECTRA * INPUTS, 2 * LANES), bf16),
            pltpu.VMEM((SPECTRA * INPUTS, 2 * LANES), jnp.float32),
            pltpu.VMEM((SPECTRA * INPUTS, LANES), jnp.float32),
            pltpu.VMEM((n_freq, 5, INPUTS, LANES), bf16),
            dma((CHUNKS,)), dma((2,)), dma((CHUNKS,)), dma((CHUNKS,)), dma((CHUNKS,)),
            dma((4, 2)), dma((4, 2)), dma((4, 2)), dma((4, 2)),
        ],
        compiler_params=pltpu.CompilerParams(
            collective_id=0, has_side_effects=True, vmem_limit_bytes=VMEM_LIMIT
        ),
    )(voltages, taps_table, dft, gains)


def correlate_kernel(n_freq, n_pair, cols, g_ref, h_ref, out_ref, x_ref, l_ref):
    channel, block = pl.program_id(0), pl.program_id(1)
    row = lax.axis_index("pair")
    lane = lax.broadcasted_iota(jnp.int32, (INPUTS, LANES), 1)
    low = lane < 64
    real_slot = (lane & 32) == 0
    zero = jnp.zeros((INPUTS, LANES), jnp.bfloat16)

    @pl.when((channel == 0) & (block == 0))
    def _():
        def gather(p, carry):
            for src in range(n_freq):
                t0, t1, t2, t3 = (g_ref[p, t, src] for t in range(4))
                t4 = h_ref[p, src // 2]
                if src % 2:
                    t4 = pltpu.roll(t4, 64, 1)
                at = pl.ds(pl.multiple_of((p * n_freq + src) * INPUTS, INPUTS), INPUTS)
                x_ref[0, at, :LANES] = jnp.where(low, t0, pltpu.roll(t1, 64, 1))
                x_ref[1, at, :LANES] = jnp.where(low, pltpu.roll(t0, 64, 1), t1)
                x_ref[2, at, :LANES] = t2
                x_ref[0, at, LANES:] = t3
                x_ref[1, at, LANES:] = t3
                x_ref[2, at, LANES:] = t4
            return carry

        lax.fori_loop(0, n_pair, gather, 0)

        def rows(src, carry):
            at = pl.ds(pl.multiple_of((row * n_freq + src) * INPUTS, INPUTS), INPUTS)
            for c in range(3):
                for k in range(2):
                    x = x_ref[c, at, k * LANES : (k + 1) * LANES]
                    if k:
                        x = jnp.where(low == (c != 1), x, zero)
                    turned = jnp.where(real_slot, pltpu.roll(x, 96, 1), -pltpu.roll(x, 32, 1))
                    to = pl.multiple_of(src * INPUTS, INPUTS)
                    l_ref[c, pl.ds(to, INPUTS), k * LANES : (k + 1) * LANES] = x
                    l_ref[c, pl.ds(n_freq * INPUTS + to, INPUTS), k * LANES : (k + 1) * LANES] = turned
            return carry

        lax.fori_loop(0, n_freq, rows, 0)

    at = pl.ds(pl.multiple_of(block * cols, cols), cols)
    sums = lax.dot_general(
        l_ref[channel], x_ref[channel, at, :], (((1,), (1,)), ((), ())), preferred_element_type=jnp.float32
    )
    sums = (sums * (1.0 / SAMPLES)).astype(jnp.bfloat16)
    out_ref[0, 0] = sums[: n_freq * INPUTS]
    out_ref[0, 1] = sums[n_freq * INPUTS :]


def correlate_call(n_freq, n_pair, spectra, packed):
    rows, columns, cols = n_freq * INPUTS, n_pair * n_freq * INPUTS, 512
    vmem = pl.BlockSpec(memory_space=pltpu.VMEM)
    return pl.pallas_call(
        functools.partial(correlate_kernel, n_freq, n_pair, cols),
        grid=(3, columns // cols),
        out_shape=jax.ShapeDtypeStruct((3, 2, rows, columns), jnp.bfloat16),
        in_specs=[vmem, vmem],
        out_specs=pl.BlockSpec((1, 2, rows, cols), lambda c, b: (c, 0, 0, b)),
        scratch_shapes=[
            pltpu.VMEM((3, columns, 2 * LANES), jnp.bfloat16),
            pltpu.VMEM((3, 2 * rows, 2 * LANES), jnp.bfloat16),
        ],
        compiler_params=pltpu.CompilerParams(vmem_limit_bytes=VMEM_LIMIT),
    )(spectra, packed)


def solution(mesh):
    n_freq, n_pair = mesh.shape["freq"], mesh.shape["pair"]
    taps_table = jnp.asarray(filter_table())
    dft = jnp.asarray(dft_table()).astype(jnp.bfloat16)

    def body(voltages, gains):
        frames = voltages.transpose(1, 0, 2)
        spectra, packed = spectra_call(n_freq, n_pair, frames, taps_table, dft, gains)
        return correlate_call(n_freq, n_pair, spectra, packed)

    placed = (P(("pair", "freq"), None, None), P(("pair", "freq"), None))
    return jax.shard_map(
        body, mesh=mesh, in_specs=placed, out_specs=P("freq", None, "pair", None), check_vma=False
    )
```

time: 171 us -> 59.9 us (0.35)
  other arithmetic: 60.6 us -> 0 us
  Pallas kernels: 0 us -> 59.7 us
  matrix products: 31.7 us -> 0 us
  waiting for transfers between devices: 30.9 us -> 0 us
  blocking collectives: 23.5 us -> 0 us
  between operations: 13.5 us -> 0.01 us
  local copies, waits for them, and re-layouts: 10.8 us -> 0 us
    convert_element_type x4 -> x0, other arithmetic: 60.2 us -> none  [the longest x1 36.5 us: body(): filtered.astype(jnp.bfloat16).reshape(local_inputs * SAMPLES, NFFT)]
    pallas_call x0 -> x2, Pallas kernels: none -> 59.7 us  [the longest x1 45.4 us: spectra_call(): pl.pallas_call(functools.partial(spectra_kernel, n_freq, n_pair), out_sha...]
    dot_general x5 -> x0, matrix products: 31.7 us -> none  [the longest x4 21.3 us: contract(): jnp.einsum('csr,csk->crk', left_side, right_side, preferred_element_type=...]
    all_gather x1 -> x0, waiting for transfers between devices: 30.9 us -> none  [body(): lax.all_gather(row_side, 'pair', axis=3, tiled=True)]
    all_to_all x1 -> x0, blocking collectives: 23.5 us -> none  [body(): lax.all_to_all(spectra, 'freq', split_axis=0, concat_axis=1, tiled=True)]
    convert_element_type x2 -> x0, local copies, waits for them, and re-layouts: 5.59 us -> none  [the longest x1 5.08 us: correlate(): return (result * (1.0 / SAMPLES)).astype(jnp.bfloat16)]
    reshape x3 -> x0, local copies, waits for them, and re-layouts: 2.44 us -> none  [the longest x2 1.75 us: body(): turned.reshape(2, ch_dev, n_freq * local_inputs, SAMPLES)]
  transfers between devices with their start and end apart: 1 -> 0, of which waited for: 1 -> 0; matrix products, arithmetic and copies ran while one was open for 0% -> 0% of each run, Pallas kernels for 0% -> 0%
where the time goes in v1:
time: 59.9 us; the launch traced here: 59.8 us
  Pallas kernels  59.7 us (100%)
    pallas_call x1, Pallas kernels, spectra_call(): pl.pallas_call(functools.partial(spectra_kernel, n_freq, n_pair), out_sha...  45.4 us
    pallas_call x1, Pallas kernels, correlate_call(): pl.pallas_call(functools.partial(correlate_kernel, n_freq, n_pair, cols),...  14.4 us

profile of v1, /device:TPU:1, one launch (start us, length us, event | category | flops | bytes accessed | tf_op | source)
XLA Modules:
  0.0 59.8 jit_solution(13680014954423297419)
XLA Ops:
  0.0 45.4 %shard_map.46 = (bf16[4,5,32,16,128]{4,3,2,1,0:T(8,128)(2,1)}, bf16[4,16,16,128]{3,2,1,0:T(8,128)(2,1)}) custom-call(s32[103,16,2048]{2,1,0:T(8,128)} %bitcast.1, f32[8,2048]{1,0:T(8,128)} %constant.4.clone.taps_hbm, bf16[2048,256]{1,0:T(8,128)(2,1)} %constant.5.clone.dft_hbm, f32[16,96]{1,0:T(8,128)} %gains_ref.1), custom_call_target="tpu_custom_call" | custom-call | tf_op jit(solution)/shard_map/pallas_call | solution.py:282
  45.4 14.4 %shard_map.47 = bf16[3,2,512,2048]{3,2,1,0:T(8,128)(2,1)} custom-call(bf16[4,5,32,16,128]{4,3,2,1,0:T(8,128)(2,1)} %get-tuple-element.7.g_ref, bf16[4,16,16,128]{3,2,1,0:T(8,128)(2,1)} %get-tuple-element.8.h_ref), custom_call_target="tpu_custom_call" | custom-call | tf_op jit(solution)/shard_map/pallas_call | solution.py:364

commit v2 on v1

v2 whole, which is shorter than its diff:
```python
import functools
import math

import jax
import jax.numpy as jnp
import numpy as np
from jax import lax
from jax.experimental import pallas as pl
from jax.experimental.pallas import tpu as pltpu
from jax.sharding import PartitionSpec as P

NFFT = 2048
TAPS = 8
SAMPLES = 96
FRAMES = 103
FIRST = 256
CHANNELS = 96
CHUNKS = 3
SPECTRA = SAMPLES // CHUNKS
INPUTS = 16
LANES = 128
GROUPS = ((0, 0), (0, 1), (1, 0), (1, 1), (2, 0), (2, 1), (2, 0), (2, 1))
SENT = ((0, 1), (1, 2), (3, 2))
VMEM_LIMIT = 36 * 1024 * 1024


def filter_table():
    positions = np.arange(TAPS * NFFT, dtype=np.float64)
    span_width = float(TAPS * NFFT)
    window = 0.5 - 0.5 * np.cos(2.0 * np.pi * (positions + 0.5) / span_width)
    taps_table = window * np.sinc((positions - span_width / 2 + 0.5) / NFFT)
    return taps_table.astype(np.float32).reshape(TAPS, NFFT)


def dft_table():
    samples = np.arange(NFFT)
    bins = FIRST + np.arange(CHANNELS)
    angles = (bins[:, None] * samples[None, :] % NFFT) * (2.0 * math.pi / NFFT)
    amplitude = 0.25 / math.sqrt(NFFT)
    tables = np.stack([np.cos(angles) * amplitude, -np.sin(angles) * amplitude])
    columns = [tables[part, channel::3] for channel, part in GROUPS]
    return np.concatenate(columns, 0).T.astype(np.float32)


def exchange_lanes(rows):
    lane = lax.broadcasted_iota(jnp.int32, rows[0].shape, 1)
    step = len(rows) // 2
    while step:
        odd = (lane & step) != 0
        out = list(rows)
        for s in range(len(rows)):
            if not s & step:
                low, high = rows[s], rows[s + step]
                out[s] = jnp.where(odd, pltpu.roll(high, step, 1), low)
                out[s + step] = jnp.where(odd, high, pltpu.roll(low, LANES - step, 1))
        rows, step = out, step // 2
    return rows


def spectra_kernel(
    n_freq, n_pair, v_hbm, taps_hbm, dft_hbm, gains_ref, x_ref, mid_ref, end_ref, x4_ref, l_ref,
    v_buf, taps_raw, taps_buf, dft_buf, gain_buf, f0, f1, y_ref, c2_ref, w_ref, t0_ref,
    v_sem, table_sem, turn_send, turn_recv, own_sem, side_send, side_recv, pass_send, pass_recv,
):
    me = lax.axis_index("freq")
    row = lax.axis_index("pair")
    right, left = lax.rem(row + 1, n_pair), lax.rem(row + n_pair - 1, n_pair)

    tables = [
        pltpu.make_async_copy(taps_hbm, taps_raw, table_sem.at[0]),
        pltpu.make_async_copy(dft_hbm, dft_buf, table_sem.at[1]),
    ]
    tables[0].start()
    history = TAPS - 1

    def first_load(piece):
        frames = pl.ds(0, SPECTRA + history)
        cols = pl.ds(pl.multiple_of(piece * (NFFT // 4), NFFT // 4), NFFT // 4)
        return pltpu.make_async_copy(
            v_hbm.at[frames, :, cols], v_buf.at[frames, :, cols], v_sem.at[piece]
        )

    def later_load(chunk):
        frames = pl.ds(chunk * SPECTRA + history, SPECTRA)
        return pltpu.make_async_copy(v_hbm.at[frames], v_buf.at[frames], v_sem.at[3 + chunk])

    for piece in range(4):
        first_load(piece).start()
        if piece == 0:
            tables[1].start()

    barrier = pltpu.get_barrier_semaphore()

    def greet(j, carry):
        pl.semaphore_signal(barrier, inc=1, device_id={"freq": lax.rem(me + j, n_freq)})
        return carry

    lax.fori_loop(1, n_freq, greet, 0)
    for side in (left, right):
        pl.semaphore_signal(barrier, inc=1, device_id={"pair": side})

    lane = lax.broadcasted_iota(jnp.int32, (CHANNELS, 2 * LANES), 1)
    chan = lax.broadcasted_iota(jnp.int32, (CHANNELS, 2 * LANES), 0)
    wanted = 3 * (lane % 32) + jnp.minimum(lane // 64, 2)
    picks = jnp.where(chan == wanted, 1.0, 0.0).astype(jnp.float32)
    gain_buf[...] = jnp.dot(
        gains_ref[...], picks, precision=lax.Precision.HIGHEST, preferred_element_type=jnp.float32
    )
    tables[0].wait()
    for t in range(TAPS):
        for n in range(NFFT // LANES):
            taps_buf[t, n] = jnp.broadcast_to(
                taps_raw[t : t + 1, n * LANES : (n + 1) * LANES], (8, LANES)
            )

    def filter_slice(chunk, q, out):
        for u in range(2):
            n = 2 * q + u
            col = pl.ds(pl.multiple_of(n * LANES, LANES), LANES)
            taps = [taps_buf[t, n] for t in range(TAPS)]

            def frame(s, half):
                return v_buf[chunk * SPECTRA + s, half * 8 : half * 8 + 8, col].astype(jnp.float32)

            window = [[frame(s, half) for s in range(TAPS)] for half in range(2)]
            for s in range(SPECTRA):
                halves = []
                for half in range(2):
                    if s > 0:
                        window[half] = window[half][1:] + [frame(s + TAPS - 1, half)]
                    terms = [taps[t] * window[half][t] for t in range(TAPS)]
                    while len(terms) > 1:
                        terms = [a + b for a, b in zip(terms[::2], terms[1::2])]
                    halves.append(terms[0])
                out[s * INPUTS : (s + 1) * INPUTS, u * LANES : (u + 1) * LANES] = jnp.concatenate(
                    halves, 0
                ).astype(jnp.bfloat16)

    def transform_slice(q, filtered, start=False):
        rows = pl.ds(pl.multiple_of(q * 2 * LANES, 2 * LANES), 2 * LANES)
        part = jnp.dot(filtered[...], dft_buf[rows, :], preferred_element_type=jnp.float32)
        if start:
            y_ref[...] = part
        else:
            y_ref[...] += part

    def channelize(chunk, serve=None):
        if chunk == 0:
            first_load(0).wait()
        else:
            later_load(chunk).wait()
        if chunk == 1:
            later_load(2).start()
        filter_slice(chunk, 0, f0)
        if chunk == 0:
            tables[1].wait()
        transform_slice(0, f0, True)
        filter_slice(chunk, 1, f1)

        def step(j, carry):
            if chunk == 0:
                first_load(j).wait()
                pl.when(j == 2)(lambda: later_load(1).start())
            if serve is not None:
                pl.when(j == 3)(serve)
            transform_slice(2 * j - 1, f1)
            filter_slice(chunk, 2 * j, f0)
            transform_slice(2 * j, f0)
            filter_slice(chunk, 2 * j + 1, f1)
            return carry

        lax.fori_loop(1, NFFT // LANES // 4, step, 0)
        transform_slice(NFFT // LANES // 2 - 1, f1)

    def rearrange(chunk):
        def spread(rows, tile):
            for f, block in enumerate(exchange_lanes(rows)):
                w_ref[f, tile] = block

        tile = SENT[chunk][0]
        at = [slice(s * INPUTS, (s + 1) * INPUTS) for s in range(SPECTRA)]
        spread([(y_ref[r, :LANES] * gain_buf[:, :LANES]).astype(jnp.bfloat16) for r in at], tile)
        if chunk == 0:
            c2_ref[...] = y_ref[:, LANES:]
            return
        lane = lax.broadcasted_iota(jnp.int32, (INPUTS, LANES), 1)
        rows = []
        for r in at:
            part = y_ref[r, LANES:]
            if chunk == 1:
                part = jnp.where(lane < 64, c2_ref[r, :], part)
            rows.append((part * gain_buf[:, LANES:]).astype(jnp.bfloat16))
        spread(rows, tile + 1)

    def landing(chunk, block):
        if chunk == 0:
            return t0_ref.at[:, block]
        return (mid_ref if chunk == 1 else end_ref).at[:, block]

    z, x, core = me // 8, lax.rem(me // 2, 4), lax.rem(me, 2)
    steps = [(dz, dx, dc) for dz in (2, 1, 3, 0) for dx in (2, 1, 3, 0) for dc in (0, 1)]
    steps.sort(key=lambda d: -min(d[0], 4 - d[0]) - min(d[1], 4 - d[1]))
    peers = [
        lax.rem(z + dz, 4) * 8 + lax.rem(x + dx, 4) * 2 + lax.rem(core + dc, 2)
        for dz, dx, dc in steps
        if dz or dx or dc
    ]

    def own_copy(chunk):
        first, tiles = SENT[chunk]
        return pltpu.make_async_copy(
            w_ref.at[me, pl.ds(first, tiles)], landing(chunk, row).at[:, me], own_sem.at[chunk]
        )

    def turn(chunk):
        first, tiles = SENT[chunk]
        for f in peers:
            pltpu.make_async_remote_copy(
                src_ref=w_ref.at[f, pl.ds(first, tiles)], dst_ref=landing(chunk, row).at[:, me],
                send_sem=turn_send.at[chunk], recv_sem=turn_recv.at[chunk], device_id={"freq": f},
            ).start()
        own_copy(chunk).start()

    def turn_bytes(chunk):
        first, tiles = SENT[chunk]
        block = w_ref.at[pl.ds(0, n_freq - 1), pl.ds(first, tiles)]
        return pltpu.make_async_remote_copy(
            src_ref=block, dst_ref=block, send_sem=turn_send.at[chunk], recv_sem=turn_recv.at[chunk],
            device_id={"freq": me},
        )

    def turned(chunk):
        turn_bytes(chunk).wait_recv()
        own_copy(chunk).wait()

    def piece(k, block, half):
        if k == 3:
            return x4_ref.at[block, pl.ds(half * n_freq // 4, n_freq // 4)]
        ref = landing(k, block).at[:, pl.ds(half * n_freq // 2, n_freq // 2)]
        return ref.at[0] if k == 2 else ref

    def side_copy(k, way, half):
        ref = piece(k, row, half)
        return pltpu.make_async_remote_copy(
            src_ref=ref, dst_ref=ref, send_sem=side_send.at[k, way, half], recv_sem=side_recv.at[k, way, half],
            device_id={"pair": right if way == 0 else left},
        )

    def pass_copy(k, way):
        ref = piece(k, left if way == 0 else right, way)
        return pltpu.make_async_remote_copy(
            src_ref=ref, dst_ref=ref, send_sem=pass_send.at[k, way], recv_sem=pass_recv.at[k, way],
            device_id={"pair": right if way == 0 else left},
        )

    def spread(*pieces):
        for first in (True, False):
            for k in pieces:
                for way in range(2):
                    side_copy(k, way, way if first else 1 - way).start()

    def forward(*pieces):
        for k in pieces:
            for way in range(2):
                side_copy(k, way, way).wait_recv()
                pass_copy(k, way).start()

    def arrived(*pieces):
        for k in pieces:
            for way in range(2):
                side_copy(k, way, 1 - way).wait_recv()

    def passed(*pieces):
        for k in pieces:
            for way in range(2):
                pass_copy(k, way).wait_recv()

    low = lax.broadcasted_iota(jnp.int32, (INPUTS, LANES), 1) < 64
    real_slot = (lax.broadcasted_iota(jnp.int32, (INPUTS, LANES), 1) & 32) == 0
    zero = jnp.zeros((INPUTS, LANES), jnp.bfloat16)

    def sort(block):
        def one(src, carry):
            t0, t1 = t0_ref[0, block, src], mid_ref[0, block, src]
            x_ref[0, block, src] = jnp.where(low, t0, pltpu.roll(t1, 64, 1))
            x_ref[1, block, src] = jnp.where(low, pltpu.roll(t0, 64, 1), t1)
            return carry

        lax.fori_loop(0, n_freq, one, 0, unroll=4)

    def put_rows(c, k, src, x):
        turned_x = jnp.where(real_slot, pltpu.roll(x, 96, 1), -pltpu.roll(x, 32, 1))
        l_ref[c, 0, src, :, k * LANES : (k + 1) * LANES] = x
        l_ref[c, 1, src, :, k * LANES : (k + 1) * LANES] = turned_x

    def rows_early():
        def one(src, carry):
            for c in range(4):
                put_rows(c, 0, src, x_ref[c, row, src] if c < 2 else mid_ref[1, row, src])
            return carry

        lax.fori_loop(0, n_freq, one, 0)

    def rows_late():
        def one(src, carry):
            t3, t4 = end_ref[0, row, src], end_ref[1, row, src]
            put_rows(0, 1, src, jnp.where(low, t3, zero))
            put_rows(1, 1, src, jnp.where(low, zero, t3))
            put_rows(2, 1, src, jnp.where(low, t4, zero))
            put_rows(3, 1, src, jnp.where(low, zero, t4))
            return carry

        lax.fori_loop(0, n_freq, one, 0)

    def after_first():
        turned(0)
        spread(0)

    def after_second():
        turned(1)
        spread(1)

    channelize(0)
    rearrange(0)
    pl.semaphore_wait(barrier, n_freq + 1)
    turn(0)
    channelize(1, after_first)
    rearrange(1)
    turn(1)
    forward(0)
    channelize(2, after_second)
    rearrange(2)
    turn(2)
    sort(row)
    rows_early()
    forward(1)
    turned(2)
    for src in range(n_freq // 2):
        x4_ref[row, src] = jnp.where(low, end_ref[1, row, src], end_ref[1, row, src + n_freq // 2])
    spread(2, 3)
    rows_late()
    arrived(0, 1)
    sort(right)
    sort(left)
    forward(2, 3)
    passed(0, 1)
    sort(lax.rem(row + 2, n_pair))
    arrived(2, 3)
    for k in range(4):
        for way in range(2):
            for half in range(2):
                side_copy(k, way, half).wait_send()
            pass_copy(k, way).wait_send()
    for chunk in range(CHUNKS):
        turn_bytes(chunk).wait_send()
    passed(2, 3)


def spectra_call(n_freq, n_pair, voltages, taps_table, dft, gains):
    bf16 = jnp.bfloat16
    anywhere = pl.BlockSpec(memory_space=pl.ANY)
    vmem = pl.BlockSpec(memory_space=pltpu.VMEM)
    dma = pltpu.SemaphoreType.DMA
    in_hbm = functools.partial(pltpu.with_memory_space_constraint, memory_space=pltpu.HBM)
    return pl.pallas_call(
        functools.partial(spectra_kernel, n_freq, n_pair),
        out_shape=(
            pltpu.VMEM((2, n_pair, n_freq, INPUTS, LANES), bf16),
            pltpu.VMEM((2, n_pair, n_freq, INPUTS, LANES), bf16),
            pltpu.VMEM((2, n_pair, n_freq, INPUTS, LANES), bf16),
            pltpu.VMEM((n_pair, n_freq // 2, INPUTS, LANES), bf16),
            pltpu.VMEM((4, 2, n_freq, INPUTS, 2 * LANES), bf16),
        ),
        in_specs=[anywhere, anywhere, anywhere, vmem],
        out_specs=(vmem,) * 5,
        scratch_shapes=[
            pltpu.VMEM((FRAMES, INPUTS, NFFT), jnp.int32),
            pltpu.VMEM((TAPS, NFFT), jnp.float32),
            pltpu.VMEM((TAPS, NFFT // LANES, 8, LANES), jnp.float32),
            pltpu.VMEM((NFFT, 2 * LANES), bf16),
            pltpu.VMEM((INPUTS, 2 * LANES), jnp.float32),
            pltpu.VMEM((SPECTRA * INPUTS, 2 * LANES), bf16),
            pltpu.VMEM((SPECTRA * INPUTS, 2 * LANES), bf16),
            pltpu.VMEM((SPECTRA * INPUTS, 2 * LANES), jnp.float32),
            pltpu.VMEM((SPECTRA * INPUTS, LANES), jnp.float32),
            pltpu.VMEM((n_freq, 5, INPUTS, LANES), bf16),
            pltpu.VMEM((1, n_pair, n_freq, INPUTS, LANES), bf16),
            dma((6,)), dma((2,)), dma((CHUNKS,)), dma((CHUNKS,)), dma((CHUNKS,)),
            dma((4, 2, 2)), dma((4, 2, 2)), dma((4, 2)), dma((4, 2)),
        ],
        compiler_params=pltpu.CompilerParams(
            collective_id=0, has_side_effects=True, vmem_limit_bytes=VMEM_LIMIT
        ),
    )(*map(in_hbm, (voltages, taps_table, dft, gains)))


def correlate_kernel(n_freq, n_pair, x_ref, mid_ref, end_ref, x4_ref, l_ref, out_hbm, out_buf, sem):
    rows, half = n_freq * INPUTS, n_freq * INPUTS // 2

    def copy(c, p):
        cols = pl.ds(pl.multiple_of(p * rows, rows), rows)
        return pltpu.make_async_copy(out_buf.at[c, p], out_hbm.at[c, :, :, cols], sem.at[c, p])

    for c in range(3):

        def block(p, carry):
            for h in range(2):
                srcs = slice(h * n_freq // 2, (h + 1) * n_freq // 2)
                first = (x_ref[c, p, srcs] if c < 2 else mid_ref[1, p, srcs]).reshape(half, LANES)
                last = (x4_ref[p] if c == 2 else end_ref[0, p, srcs]).reshape(half, LANES)
                side = l_ref[3 if c == 2 and h else c].reshape(2 * rows, 2 * LANES)
                sums = lax.dot_general(
                    side, jnp.concatenate([first, last], 1), (((1,), (1,)), ((), ())),
                    preferred_element_type=jnp.float32,
                )
                sums = (sums * (1.0 / SAMPLES)).astype(jnp.bfloat16)
                out_buf[c, p, 0, :, h * half : (h + 1) * half] = sums[:rows]
                out_buf[c, p, 1, :, h * half : (h + 1) * half] = sums[rows:]
            copy(c, p).start()
            return carry

        lax.fori_loop(0, n_pair, block, 0, unroll=True)

    for c in range(3):
        for p in range(n_pair):
            copy(c, p).wait()


def correlate_call(n_freq, n_pair, *spectra):
    rows, columns = n_freq * INPUTS, n_pair * n_freq * INPUTS
    vmem = pl.BlockSpec(memory_space=pltpu.VMEM)
    return pl.pallas_call(
        functools.partial(correlate_kernel, n_freq, n_pair),
        out_shape=jax.ShapeDtypeStruct((3, 2, rows, columns), jnp.bfloat16),
        in_specs=[vmem] * 5,
        out_specs=pl.BlockSpec(memory_space=pl.ANY),
        scratch_shapes=[
            pltpu.VMEM((3, n_pair, 2, rows, rows), jnp.bfloat16),
            pltpu.SemaphoreType.DMA((3, n_pair)),
        ],
        compiler_params=pltpu.CompilerParams(vmem_limit_bytes=VMEM_LIMIT),
    )(*(pltpu.with_memory_space_constraint(x, pltpu.VMEM) for x in spectra))


def solution(mesh):
    n_freq, n_pair = mesh.shape["freq"], mesh.shape["pair"]
    taps_table = jnp.asarray(filter_table())
    dft = jnp.asarray(dft_table()).astype(jnp.bfloat16)

    def body(voltages, gains):
        frames = voltages.transpose(1, 0, 2)
        return correlate_call(n_freq, n_pair, *spectra_call(n_freq, n_pair, frames, taps_table, dft, gains))

    placed = (P(("pair", "freq"), None, None), P(("pair", "freq"), None))
    return jax.shard_map(
        body, mesh=mesh, in_specs=placed, out_specs=P("freq", None, "pair", None), check_vma=False
    )
```

time: 59.9 us -> 46.7 us (0.78)
  Pallas kernels: 59.7 us -> 46.6 us
    pallas_call x1, Pallas kernels: 14.4 us -> 5.14 us  [correlate_call(): pl.pallas_call(functools.partial(correlate_kernel, n_freq, n_pair), out_s...]
    pallas_call x1, Pallas kernels: 45.4 us -> 41.4 us  [spectra_call(): pl.pallas_call(functools.partial(spectra_kernel, n_freq, n_pair), out_sha...]
where the time goes in v2:
time: 46.7 us; the launch traced here: 46.6 us
  Pallas kernels  46.6 us (100%)
    pallas_call x1, Pallas kernels, spectra_call(): pl.pallas_call(functools.partial(spectra_kernel, n_freq, n_pair), out_sha...  41.4 us
    pallas_call x1, Pallas kernels, correlate_call(): pl.pallas_call(functools.partial(correlate_kernel, n_freq, n_pair), out_s...  5.14 us

profile of v2, /device:TPU:1, one launch (start us, length us, event | category | flops | bytes accessed | tf_op | source)
XLA Modules:
  0.0 46.6 jit_solution(2540718016748288256)
XLA Ops:
  0.0 41.4 %shard_map.46 = (bf16[2,4,32,16,128]{4,3,2,1,0:T(8,128)(2,1)S(1)}, bf16[2,4,32,16,128]{4,3,2,1,0:T(8,128)(2,1)S(1)}, bf16[2,4,32,16,128]{4,3,2,1,0:T(8,128)(2,1)...) custom-call(s32[103,16,2048]{2,1,0:T(8,128)} %bitcast.1, f32[8,2048]{1,0:T(8,128)} %constant.4.clone.taps_hbm, ...), custom_call_target="tpu_custom_call" | custom-call | tf_op jit(solution)/shard_map/pallas_call | solution.py:365
  41.5 5.1 %shard_map.47 = bf16[3,2,512,2048]{3,2,1,0:T(8,128)(2,1)} custom-call(bf16[2,4,32,16,128]{4,3,2,1,0:T(8,128)(2,1)S(1)} %get-tuple-element.10.x_ref, bf16[2,4,32,16,128]{4,3,2,1,0:T(8,128)(2,1)S(1)} %get-tuple-element.11.mid_ref, bf16[2,4,32,16,128]{4,3,2,1,0:T(8,128)(2,1)S(1)} %get-tuple-element.12.end_ref, ...), custom_call_target="tpu_custom_call" | custom-call | tf_op jit(solution)/shard_map/pallas_call | solution.py:432

commit v3 on v2

--- a/solution.py
+++ b/solution.py
@@ -58,9 +58,9 @@
 
 
 def spectra_kernel(
-    n_freq, n_pair, v_hbm, taps_hbm, dft_hbm, gains_ref, x_ref, mid_ref, end_ref, x4_ref, l_ref,
-    v_buf, taps_raw, taps_buf, dft_buf, gain_buf, f0, f1, y_ref, c2_ref, w_ref, t0_ref,
-    v_sem, table_sem, turn_send, turn_recv, own_sem, side_send, side_recv, pass_send, pass_recv,
+    n_freq, n_pair, v_hbm, taps_hbm, dft_hbm, gains_hbm, x_out, mid_out, end_out, x4_out, l_out,
+    v_buf, gains_ref, taps_raw, taps_buf, dft_buf, gain_buf, f0, f1, y_ref, c2_ref, w_ref, t0_ref, x_ref, mid_ref, end_ref, x4_ref, l_ref,
+    v_sem, table_sem, turn_send, turn_recv, own_sem, out_sem, side_send, side_recv, pass_send, pass_recv,
 ):
     me = lax.axis_index("freq")
     row = lax.axis_index("pair")
@@ -69,6 +69,7 @@
     tables = [
         pltpu.make_async_copy(taps_hbm, taps_raw, table_sem.at[0]),
         pltpu.make_async_copy(dft_hbm, dft_buf, table_sem.at[1]),
+        pltpu.make_async_copy(gains_hbm, gains_ref, table_sem.at[2]),
     ]
     tables[0].start()
     history = TAPS - 1
@@ -84,10 +85,10 @@
         frames = pl.ds(chunk * SPECTRA + history, SPECTRA)
         return pltpu.make_async_copy(v_hbm.at[frames], v_buf.at[frames], v_sem.at[3 + chunk])
 
-    for piece in range(4):
-        first_load(piece).start()
-        if piece == 0:
-            tables[1].start()
+    first_load(0).start()
+    tables[1].start()
+    tables[2].start()
+    first_load(1).start()
 
     barrier = pltpu.get_barrier_semaphore()
 
@@ -99,13 +100,6 @@
     for side in (left, right):
         pl.semaphore_signal(barrier, inc=1, device_id={"pair": side})
 
-    lane = lax.broadcasted_iota(jnp.int32, (CHANNELS, 2 * LANES), 1)
-    chan = lax.broadcasted_iota(jnp.int32, (CHANNELS, 2 * LANES), 0)
-    wanted = 3 * (lane % 32) + jnp.minimum(lane // 64, 2)
-    picks = jnp.where(chan == wanted, 1.0, 0.0).astype(jnp.float32)
-    gain_buf[...] = jnp.dot(
-        gains_ref[...], picks, precision=lax.Precision.HIGHEST, preferred_element_type=jnp.float32
-    )
     tables[0].wait()
     for t in range(TAPS):
         for n in range(NFFT // LANES):
@@ -144,9 +138,10 @@
         else:
             y_ref[...] += part
 
-    def channelize(chunk, serve=None):
+    def channelize(chunk, serve=()):
         if chunk == 0:
             first_load(0).wait()
+            first_load(2).start()
         else:
             later_load(chunk).wait()
         if chunk == 1:
@@ -160,9 +155,10 @@
         def step(j, carry):
             if chunk == 0:
                 first_load(j).wait()
+                pl.when(j == 1)(lambda: first_load(3).start())
                 pl.when(j == 2)(lambda: later_load(1).start())
-            if serve is not None:
-                pl.when(j == 3)(serve)
+            for when, who, what in serve:
+                pl.when((j == when) & who)(what)
             transform_slice(2 * j - 1, f1)
             filter_slice(chunk, 2 * j, f0)
             transform_slice(2 * j, f0)
@@ -171,6 +167,16 @@
 
         lax.fori_loop(1, NFFT // LANES // 4, step, 0)
         transform_slice(NFFT // LANES // 2 - 1, f1)
+
+    def order_gains():
+        tables[2].wait()
+        lane = lax.broadcasted_iota(jnp.int32, (CHANNELS, 2 * LANES), 1)
+        chan = lax.broadcasted_iota(jnp.int32, (CHANNELS, 2 * LANES), 0)
+        wanted = 3 * (lane % 32) + jnp.minimum(lane // 64, 2)
+        picks = jnp.where(chan == wanted, 1.0, 0.0).astype(jnp.float32)
+        gain_buf[...] = jnp.dot(
+            gains_ref[...], picks, precision=lax.Precision.HIGHEST, preferred_element_type=jnp.float32
+        )
 
     def rearrange(chunk):
         def spread(rows, tile):
@@ -193,9 +199,9 @@
         spread(rows, tile + 1)
 
     def landing(chunk, block):
-        if chunk == 0:
-            return t0_ref.at[:, block]
-        return (mid_ref if chunk == 1 else end_ref).at[:, block]
+        if chunk == 2:
+            return end_ref
+        return (mid_ref if chunk == 1 else t0_ref).at[:, block]
 
     z, x, core = me // 8, lax.rem(me // 2, 4), lax.rem(me, 2)
     steps = [(dz, dx, dc) for dz in (2, 1, 3, 0) for dx in (2, 1, 3, 0) for dc in (0, 1)]
@@ -217,32 +223,46 @@
         for f in peers:
             pltpu.make_async_remote_copy(
                 src_ref=w_ref.at[f, pl.ds(first, tiles)], dst_ref=landing(chunk, row).at[:, me],
-                send_sem=turn_send.at[chunk], recv_sem=turn_recv.at[chunk], device_id={"freq": f},
+                send_sem=turn_send.at[chunk], recv_sem=turn_recv.at[chunk, my_half], device_id={"freq": f},
             ).start()
         own_copy(chunk).start()
 
-    def turn_bytes(chunk):
+    my_half = me // (n_freq // 2)
+    early = my_half == 0
+    late = my_half == 1
+
+    def turn_bytes(chunk, half, count):
         first, tiles = SENT[chunk]
-        block = w_ref.at[pl.ds(0, n_freq - 1), pl.ds(first, tiles)]
+        block = w_ref.at[pl.ds(0, count), pl.ds(first, tiles)]
         return pltpu.make_async_remote_copy(
-            src_ref=block, dst_ref=block, send_sem=turn_send.at[chunk], recv_sem=turn_recv.at[chunk],
+            src_ref=block, dst_ref=block, send_sem=turn_send.at[chunk], recv_sem=turn_recv.at[chunk, half],
             device_id={"freq": me},
         )
 
-    def turned(chunk):
-        turn_bytes(chunk).wait_recv()
-        own_copy(chunk).wait()
+    def turned(chunk, half):
+        @pl.when(my_half == half)
+        def _():
+            turn_bytes(chunk, half, n_freq // 2 - 1).wait_recv()
+            own_copy(chunk).wait()
+
+        @pl.when(my_half != half)
+        def _():
+            turn_bytes(chunk, half, n_freq // 2).wait_recv()
+
+    def part(k, half):
+        size = n_freq // 4 if k == 3 else n_freq // 2
+        return pl.ds(half * size, size)
 
     def piece(k, block, half):
-        if k == 3:
-            return x4_ref.at[block, pl.ds(half * n_freq // 4, n_freq // 4)]
-        ref = landing(k, block).at[:, pl.ds(half * n_freq // 2, n_freq // 2)]
-        return ref.at[0] if k == 2 else ref
+        if k > 1:
+            return (end_out if k == 2 else x4_out).at[block, part(k, half)]
+        return landing(k, block).at[:, part(k, half)]
 
     def side_copy(k, way, half):
-        ref = piece(k, row, half)
+        to = piece(k, row, half)
+        ref = to if k < 2 else (end_ref.at[0] if k == 2 else x4_ref).at[part(k, half)]
         return pltpu.make_async_remote_copy(
-            src_ref=ref, dst_ref=ref, send_sem=side_send.at[k, way, half], recv_sem=side_recv.at[k, way, half],
+            src_ref=ref, dst_ref=to, send_sem=side_send.at[k, way, half], recv_sem=side_recv.at[k, way, half],
             device_id={"pair": right if way == 0 else left},
         )
 
@@ -253,17 +273,15 @@
             device_id={"pair": right if way == 0 else left},
         )
 
-    def spread(*pieces):
-        for first in (True, False):
-            for k in pieces:
-                for way in range(2):
-                    side_copy(k, way, way if first else 1 - way).start()
-
-    def forward(*pieces):
+    def spread(half, *pieces):
         for k in pieces:
             for way in range(2):
-                side_copy(k, way, way).wait_recv()
-                pass_copy(k, way).start()
+                side_copy(k, way, half).start()
+
+    def forward(way, *pieces):
+        for k in pieces:
+            side_copy(k, way, way).wait_recv()
+            pass_copy(k, way).start()
 
     def arrived(*pieces):
         for k in pieces:
@@ -288,6 +306,17 @@
 
         lax.fori_loop(0, n_freq, one, 0, unroll=4)
 
+    def keep(k, block=0):
+        if k == 0:
+            pair = x_ref.at[:, block], x_out.at[:, block]
+        elif k == 1:
+            pair = mid_ref.at[1, block], mid_out.at[block]
+        elif k == 2:
+            pair = end_ref.at[0], end_out.at[row]
+        else:
+            pair = (x4_ref, x4_out.at[row]) if k == 3 else (l_ref, l_out)
+        return pltpu.make_async_copy(*pair, out_sem.at[k, block])
+
     def put_rows(c, k, src, x):
         turned_x = jnp.where(real_slot, pltpu.roll(x, 96, 1), -pltpu.roll(x, 32, 1))
         l_ref[c, 0, src, :, k * LANES : (k + 1) * LANES] = x
@@ -303,7 +332,7 @@
 
     def rows_late():
         def one(src, carry):
-            t3, t4 = end_ref[0, row, src], end_ref[1, row, src]
+            t3, t4 = end_ref[0, src], end_ref[1, src]
             put_rows(0, 1, src, jnp.where(low, t3, zero))
             put_rows(1, 1, src, jnp.where(low, zero, t3))
             put_rows(2, 1, src, jnp.where(low, t4, zero))
@@ -312,39 +341,65 @@
 
         lax.fori_loop(0, n_freq, one, 0)
 
-    def after_first():
-        turned(0)
-        spread(0)
-
-    def after_second():
-        turned(1)
-        spread(1)
-
+    def turn_and_spread(chunk, half):
+        turned(chunk, half)
+        if chunk == 2:
+            for j in range(n_freq // 4):
+                src = half * n_freq // 2 + j
+                x4_ref[half * n_freq // 4 + j] = jnp.where(low, end_ref[1, src], end_ref[1, src + n_freq // 4])
+            spread(half, 2, 3)
+        else:
+            spread(half, chunk)
+
+    def finish(block):
+        sort(block)
+        keep(0, block).start()
+        keep(1, block).start()
+
+    take = functools.partial(functools.partial, turn_and_spread)
     channelize(0)
+    order_gains()
     rearrange(0)
     pl.semaphore_wait(barrier, n_freq + 1)
     turn(0)
-    channelize(1, after_first)
+    channelize(1, [(1, late, take(0, 0)), (3, late, take(0, 1))])
+    pl.when(early)(take(0, 0))
     rearrange(1)
     turn(1)
-    forward(0)
-    channelize(2, after_second)
+    pl.when(early)(take(0, 1))
+
+    def between():
+        forward(0, 0)
+        forward(1, 0)
+        turn_and_spread(1, 0)
+
+    channelize(2, [(2, late, between), (3, late, take(1, 1)), (2, early, lambda: forward(0, 0))])
+
+    @pl.when(early)
+    def _():
+        forward(1, 0)
+        turn_and_spread(1, 0)
+
     rearrange(2)
     turn(2)
-    sort(row)
+    pl.when(early)(take(1, 1))
+    finish(row)
     rows_early()
-    forward(1)
-    turned(2)
-    for src in range(n_freq // 2):
-        x4_ref[row, src] = jnp.where(low, end_ref[1, row, src], end_ref[1, row, src + n_freq // 2])
-    spread(2, 3)
+    turn_and_spread(2, 0)
+    forward(0, 1)
+    turn_and_spread(2, 1)
+    forward(1, 1)
+    keep(2).start()
+    keep(3).start()
     rows_late()
+    keep(4).start()
     arrived(0, 1)
-    sort(right)
-    sort(left)
-    forward(2, 3)
+    forward(0, 2, 3)
+    finish(right)
+    finish(left)
+    forward(1, 2, 3)
     passed(0, 1)
-    sort(lax.rem(row + 2, n_pair))
+    finish(lax.rem(row + 2, n_pair))
     arrived(2, 3)
     for k in range(4):
         for way in range(2):
@@ -352,29 +407,32 @@
                 side_copy(k, way, half).wait_send()
             pass_copy(k, way).wait_send()
     for chunk in range(CHUNKS):
-        turn_bytes(chunk).wait_send()
+        turn_bytes(chunk, 0, n_freq - 1).wait_send()
+    for k in range(5):
+        for block in range(n_pair if k < 2 else 1):
+            keep(k, block).wait()
     passed(2, 3)
 
 
 def spectra_call(n_freq, n_pair, voltages, taps_table, dft, gains):
     bf16 = jnp.bfloat16
     anywhere = pl.BlockSpec(memory_space=pl.ANY)
-    vmem = pl.BlockSpec(memory_space=pltpu.VMEM)
     dma = pltpu.SemaphoreType.DMA
     in_hbm = functools.partial(pltpu.with_memory_space_constraint, memory_space=pltpu.HBM)
     return pl.pallas_call(
         functools.partial(spectra_kernel, n_freq, n_pair),
         out_shape=(
             pltpu.VMEM((2, n_pair, n_freq, INPUTS, LANES), bf16),
-            pltpu.VMEM((2, n_pair, n_freq, INPUTS, LANES), bf16),
-            pltpu.VMEM((2, n_pair, n_freq, INPUTS, LANES), bf16),
+            pltpu.VMEM((n_pair, n_freq, INPUTS, LANES), bf16),
+            pltpu.VMEM((n_pair, n_freq, INPUTS, LANES), bf16),
             pltpu.VMEM((n_pair, n_freq // 2, INPUTS, LANES), bf16),
             pltpu.VMEM((4, 2, n_freq, INPUTS, 2 * LANES), bf16),
         ),
-        in_specs=[anywhere, anywhere, anywhere, vmem],
-        out_specs=(vmem,) * 5,
+        in_specs=[anywhere] * 4,
+        out_specs=(anywhere,) * 5,
         scratch_shapes=[
             pltpu.VMEM((FRAMES, INPUTS, NFFT), jnp.int32),
+            pltpu.VMEM((INPUTS, CHANNELS), jnp.float32),
             pltpu.VMEM((TAPS, NFFT), jnp.float32),
             pltpu.VMEM((TAPS, NFFT // LANES, 8, LANES), jnp.float32),
             pltpu.VMEM((NFFT, 2 * LANES), bf16),
@@ -385,7 +443,12 @@
             pltpu.VMEM((SPECTRA * INPUTS, LANES), jnp.float32),
             pltpu.VMEM((n_freq, 5, INPUTS, LANES), bf16),
             pltpu.VMEM((1, n_pair, n_freq, INPUTS, LANES), bf16),
-            dma((6,)), dma((2,)), dma((CHUNKS,)), dma((CHUNKS,)), dma((CHUNKS,)),
+            pltpu.VMEM((2, n_pair, n_freq, INPUTS, LANES), bf16),
+            pltpu.VMEM((2, n_pair, n_freq, INPUTS, LANES), bf16),
+            pltpu.VMEM((2, n_freq, INPUTS, LANES), bf16),
+            pltpu.VMEM((n_freq // 2, INPUTS, LANES), bf16),
+            pltpu.VMEM((4, 2, n_freq, INPUTS, 2 * LANES), bf16),
+            dma((6,)), dma((3,)), dma((CHUNKS,)), dma((CHUNKS, 2)), dma((CHUNKS,)), dma((5, n_pair)),
             dma((4, 2, 2)), dma((4, 2, 2)), dma((4, 2)), dma((4, 2)),
         ],
         compiler_params=pltpu.CompilerParams(
@@ -405,17 +468,25 @@
 
         def block(p, carry):
             for h in range(2):
-                srcs = slice(h * n_freq // 2, (h + 1) * n_freq // 2)
-                first = (x_ref[c, p, srcs] if c < 2 else mid_ref[1, p, srcs]).reshape(half, LANES)
-                last = (x4_ref[p] if c == 2 else end_ref[0, p, srcs]).reshape(half, LANES)
+                quarters = (2 * h, 2 * h + 1) if c < 2 else (h, h + 2)
+                spans = [slice(q * n_freq // 4, (q + 1) * n_freq // 4) for q in quarters]
+                if c < 2:
+                    first, last = ([ref[p, at] for at in spans] for ref in (x_ref.at[c], end_ref))
+                    last = jnp.concatenate(last, 0)
+                else:
+                    first, last = [mid_ref[p, at] for at in spans], x4_ref[p]
+                first = jnp.concatenate(first, 0).reshape(half, LANES)
                 side = l_ref[3 if c == 2 and h else c].reshape(2 * rows, 2 * LANES)
                 sums = lax.dot_general(
-                    side, jnp.concatenate([first, last], 1), (((1,), (1,)), ((), ())),
+                    side, jnp.concatenate([first, last.reshape(half, LANES)], 1), (((1,), (1,)), ((), ())),
                     preferred_element_type=jnp.float32,
                 )
                 sums = (sums * (1.0 / SAMPLES)).astype(jnp.bfloat16)
-                out_buf[c, p, 0, :, h * half : (h + 1) * half] = sums[:rows]
-                out_buf[c, p, 1, :, h * half : (h + 1) * half] = sums[rows:]
+                wide = half // 2
+                for k, q in enumerate(quarters):
+                    part = sums[:, k * wide : (k + 1) * wide]
+                    out_buf[c, p, 0, :, q * wide : (q + 1) * wide] = part[:rows]
+                    out_buf[c, p, 1, :, q * wide : (q + 1) * wide] = part[rows:]
             copy(c, p).start()
             return carry
 

time: 46.7 us -> 44.9 us (0.961)
  Pallas kernels: 46.6 us -> 44.8 us
    pallas_call x1, Pallas kernels: 41.4 us -> 39.7 us  [spectra_call(): pl.pallas_call(functools.partial(spectra_kernel, n_freq, n_pair), out_sha...]
where the time goes in v3:
time: 44.9 us; the launch traced here: 44.8 us
  Pallas kernels  44.8 us (100%)
    pallas_call x1, Pallas kernels, spectra_call(): pl.pallas_call(functools.partial(spectra_kernel, n_freq, n_pair), out_sha...  39.7 us
    pallas_call x1, Pallas kernels, correlate_call(): pl.pallas_call(functools.partial(correlate_kernel, n_freq, n_pair), out_s...  5.14 us

profile of v3, /device:TPU:1, one launch (start us, length us, event | category | flops | bytes accessed | tf_op | source)
XLA Modules:
  0.0 44.8 jit_solution(3287656184900888606)
XLA Ops:
  0.0 39.7 %shard_map.46 = (bf16[2,4,32,16,128]{4,3,2,1,0:T(8,128)(2,1)S(1)}, bf16[4,32,16,128]{3,2,1,0:T(8,128)(2,1)S(1)}, bf16[4,32,16,128]{3,2,1,0:T(8,128)(2,1)S(1)}, b...) custom-call(s32[103,16,2048]{2,1,0:T(8,128)} %bitcast.1, f32[8,2048]{1,0:T(8,128)} %constant.4.clone.taps_hbm, ...), custom_call_target="tpu_custom_call" | custom-call | tf_op jit(solution)/shard_map/pallas_call | solution.py:422
  39.7 5.1 %shard_map.47 = bf16[3,2,512,2048]{3,2,1,0:T(8,128)(2,1)} custom-call(bf16[2,4,32,16,128]{4,3,2,1,0:T(8,128)(2,1)S(1)} %get-tuple-element.10.x_ref, bf16[4,32,16,128]{3,2,1,0:T(8,128)(2,1)S(1)} %get-tuple-element.11.mid_ref, bf16[4,32,16,128]{3,2,1,0:T(8,128)(2,1)S(1)} %get-tuple-element.12.end_ref, bf16[4,16,16,128]{3,2,1,0:T(8,128)(2,1)S(1)} %get-tuple-element.13.x4_ref, ...), custom_call_target="tpu_custom_call" | custom-call | tf_op jit(solution)/shard_map/pallas_call | solution.py:503

commit v4 on v3

--- a/solution.py
+++ b/solution.py
@@ -20,7 +20,7 @@
 INPUTS = 16
 LANES = 128
 GROUPS = ((0, 0), (0, 1), (1, 0), (1, 1), (2, 0), (2, 1), (2, 0), (2, 1))
-SENT = ((0, 1), (1, 2), (3, 2))
+SENT = ((0, 2), (2, 1), (3, 2))
 VMEM_LIMIT = 36 * 1024 * 1024
 
 
@@ -186,14 +186,14 @@
         tile = SENT[chunk][0]
         at = [slice(s * INPUTS, (s + 1) * INPUTS) for s in range(SPECTRA)]
         spread([(y_ref[r, :LANES] * gain_buf[:, :LANES]).astype(jnp.bfloat16) for r in at], tile)
-        if chunk == 0:
+        if chunk == 1:
             c2_ref[...] = y_ref[:, LANES:]
             return
         lane = lax.broadcasted_iota(jnp.int32, (INPUTS, LANES), 1)
         rows = []
         for r in at:
             part = y_ref[r, LANES:]
-            if chunk == 1:
+            if chunk == 2:
                 part = jnp.where(lane < 64, c2_ref[r, :], part)
             rows.append((part * gain_buf[:, LANES:]).astype(jnp.bfloat16))
         spread(rows, tile + 1)
@@ -249,49 +249,51 @@
         def _():
             turn_bytes(chunk, half, n_freq // 2).wait_recv()
 
-    def part(k, half):
-        size = n_freq // 4 if k == 3 else n_freq // 2
-        return pl.ds(half * size, size)
-
-    def piece(k, block, half):
-        if k > 1:
-            return (end_out if k == 2 else x4_out).at[block, part(k, half)]
-        return landing(k, block).at[:, part(k, half)]
-
-    def side_copy(k, way, half):
-        to = piece(k, row, half)
-        ref = to if k < 2 else (end_ref.at[0] if k == 2 else x4_ref).at[part(k, half)]
+    def part(k, quarter):
+        size = n_freq // 8 if k == 3 else n_freq // 4
+        return pl.ds(quarter * size, size)
+
+    def piece(k, block, quarter):
+        ref = (t0_ref.at[0], mid_ref.at[0], end_out, x4_out, mid_out)[k]
+        return ref.at[block, part(k, quarter)]
+
+    def side_copy(k, way, quarter):
+        to = piece(k, row, quarter)
+        ref = to if k < 2 else (end_ref.at[0], x4_ref, end_ref.at[1])[k - 2].at[part(k, quarter)]
         return pltpu.make_async_remote_copy(
-            src_ref=ref, dst_ref=to, send_sem=side_send.at[k, way, half], recv_sem=side_recv.at[k, way, half],
+            src_ref=ref, dst_ref=to, send_sem=side_send.at[k, way, quarter], recv_sem=side_recv.at[k, way, quarter],
             device_id={"pair": right if way == 0 else left},
         )
 
-    def pass_copy(k, way):
-        ref = piece(k, left if way == 0 else right, way)
+    def pass_copy(k, way, half):
+        ref = piece(k, left if way == 0 else right, 2 * half + way)
         return pltpu.make_async_remote_copy(
-            src_ref=ref, dst_ref=ref, send_sem=pass_send.at[k, way], recv_sem=pass_recv.at[k, way],
+            src_ref=ref, dst_ref=ref, send_sem=pass_send.at[k, way, half], recv_sem=pass_recv.at[k, way, half],
             device_id={"pair": right if way == 0 else left},
         )
 
-    def spread(half, *pieces):
+    def spread(half, handed_on, *pieces):
         for k in pieces:
             for way in range(2):
-                side_copy(k, way, half).start()
-
-    def forward(way, *pieces):
+                side_copy(k, way, 2 * half + (way if handed_on else 1 - way)).start()
+
+    def forward(half, *pieces):
         for k in pieces:
-            side_copy(k, way, way).wait_recv()
-            pass_copy(k, way).start()
+            for way in range(2):
+                side_copy(k, way, 2 * half + way).wait_recv()
+                pass_copy(k, way, half).start()
 
     def arrived(*pieces):
         for k in pieces:
             for way in range(2):
-                side_copy(k, way, 1 - way).wait_recv()
+                for half in range(2):
+                    side_copy(k, way, 2 * half + 1 - way).wait_recv()
 
     def passed(*pieces):
         for k in pieces:
             for way in range(2):
-                pass_copy(k, way).wait_recv()
+                for half in range(2):
+                    pass_copy(k, way, half).wait_recv()
 
     low = lax.broadcasted_iota(jnp.int32, (INPUTS, LANES), 1) < 64
     real_slot = (lax.broadcasted_iota(jnp.int32, (INPUTS, LANES), 1) & 32) == 0
@@ -304,13 +306,13 @@
             x_ref[1, block, src] = jnp.where(low, pltpu.roll(t0, 64, 1), t1)
             return carry
 
-        lax.fori_loop(0, n_freq, one, 0, unroll=4)
+        lax.fori_loop(0, n_freq, one, 0, unroll=8)
 
     def keep(k, block=0):
         if k == 0:
             pair = x_ref.at[:, block], x_out.at[:, block]
         elif k == 1:
-            pair = mid_ref.at[1, block], mid_out.at[block]
+            pair = end_ref.at[1], mid_out.at[row]
         elif k == 2:
             pair = end_ref.at[0], end_out.at[row]
         else:
@@ -324,37 +326,45 @@
 
     def rows_early():
         def one(src, carry):
-            for c in range(4):
-                put_rows(c, 0, src, x_ref[c, row, src] if c < 2 else mid_ref[1, row, src])
+            for c in range(2):
+                put_rows(c, 0, src, x_ref[c, row, src])
+            t1 = t0_ref[1, row, src]
+            put_rows(2, 1, src, jnp.where(low, t1, zero))
+            put_rows(3, 1, src, jnp.where(low, zero, t1))
             return carry
 
-        lax.fori_loop(0, n_freq, one, 0)
+        lax.fori_loop(0, n_freq, one, 0, unroll=8)
 
     def rows_late():
         def one(src, carry):
             t3, t4 = end_ref[0, src], end_ref[1, src]
             put_rows(0, 1, src, jnp.where(low, t3, zero))
             put_rows(1, 1, src, jnp.where(low, zero, t3))
-            put_rows(2, 1, src, jnp.where(low, t4, zero))
-            put_rows(3, 1, src, jnp.where(low, zero, t4))
+            put_rows(2, 0, src, t4)
+            put_rows(3, 0, src, t4)
             return carry
 
-        lax.fori_loop(0, n_freq, one, 0)
+        lax.fori_loop(0, n_freq, one, 0, unroll=8)
 
     def turn_and_spread(chunk, half):
         turned(chunk, half)
         if chunk == 2:
+            spread(half, True, 2, 4)
+        elif chunk == 1:
+            spread(half, True, 1)
+            spread(half, False, 1)
+        else:
+            spread(half, True, 0)
             for j in range(n_freq // 4):
                 src = half * n_freq // 2 + j
-                x4_ref[half * n_freq // 4 + j] = jnp.where(low, end_ref[1, src], end_ref[1, src + n_freq // 4])
-            spread(half, 2, 3)
-        else:
-            spread(half, chunk)
+                pair = t0_ref[1, row, src], t0_ref[1, row, src + n_freq // 4]
+                x4_ref[half * n_freq // 4 + j] = jnp.where(low, *pair)
+            spread(half, True, 3)
+            spread(half, False, 0, 3)
 
     def finish(block):
         sort(block)
         keep(0, block).start()
-        keep(1, block).start()
 
     take = functools.partial(functools.partial, turn_and_spread)
     channelize(0)
@@ -367,51 +377,55 @@
     rearrange(1)
     turn(1)
     pl.when(early)(take(0, 1))
+    pl.when(late)(lambda: forward(0, 0, 3))
 
     def between():
-        forward(0, 0)
-        forward(1, 0)
+        forward(1, 0, 3)
         turn_and_spread(1, 0)
 
-    channelize(2, [(2, late, between), (3, late, take(1, 1)), (2, early, lambda: forward(0, 0))])
+    channelize(2, [(2, late, between), (3, late, take(1, 1)), (2, early, lambda: forward(0, 0, 3))])
 
     @pl.when(early)
     def _():
-        forward(1, 0)
+        forward(1, 0, 3)
         turn_and_spread(1, 0)
 
     rearrange(2)
     turn(2)
     pl.when(early)(take(1, 1))
+    forward(0, 1)
+    turn_and_spread(2, 0)
+    spread(0, False, 2, 4)
+    forward(1, 1)
+    turn_and_spread(2, 1)
+    spread(1, False, 2, 4)
     finish(row)
     rows_early()
-    turn_and_spread(2, 0)
-    forward(0, 1)
-    turn_and_spread(2, 1)
-    forward(1, 1)
+    keep(1).start()
     keep(2).start()
     keep(3).start()
     rows_late()
     keep(4).start()
-    arrived(0, 1)
-    forward(0, 2, 3)
+    arrived(0, 1, 3)
     finish(right)
+    forward(0, 2, 4)
     finish(left)
-    forward(1, 2, 3)
-    passed(0, 1)
+    forward(1, 2, 4)
+    passed(0, 1, 3)
     finish(lax.rem(row + 2, n_pair))
-    arrived(2, 3)
-    for k in range(4):
+    arrived(2, 4)
+    for k in range(5):
         for way in range(2):
+            for quarter in range(4):
+                side_copy(k, way, quarter).wait_send()
             for half in range(2):
-                side_copy(k, way, half).wait_send()
-            pass_copy(k, way).wait_send()
+                pass_copy(k, way, half).wait_send()
     for chunk in range(CHUNKS):
         turn_bytes(chunk, 0, n_freq - 1).wait_send()
     for k in range(5):
-        for block in range(n_pair if k < 2 else 1):
+        for block in range(n_pair if k == 0 else 1):
             keep(k, block).wait()
-    passed(2, 3)
+    passed(2, 4)
 
 
 def spectra_call(n_freq, n_pair, voltages, taps_table, dft, gains):
@@ -442,14 +456,14 @@
             pltpu.VMEM((SPECTRA * INPUTS, 2 * LANES), jnp.float32),
             pltpu.VMEM((SPECTRA * INPUTS, LANES), jnp.float32),
             pltpu.VMEM((n_freq, 5, INPUTS, LANES), bf16),
-            pltpu.VMEM((1, n_pair, n_freq, INPUTS, LANES), bf16),
             pltpu.VMEM((2, n_pair, n_freq, INPUTS, LANES), bf16),
             pltpu.VMEM((2, n_pair, n_freq, INPUTS, LANES), bf16),
+            pltpu.VMEM((1, n_pair, n_freq, INPUTS, LANES), bf16),
             pltpu.VMEM((2, n_freq, INPUTS, LANES), bf16),
             pltpu.VMEM((n_freq // 2, INPUTS, LANES), bf16),
             pltpu.VMEM((4, 2, n_freq, INPUTS, 2 * LANES), bf16),
             dma((6,)), dma((3,)), dma((CHUNKS,)), dma((CHUNKS, 2)), dma((CHUNKS,)), dma((5, n_pair)),
-            dma((4, 2, 2)), dma((4, 2, 2)), dma((4, 2)), dma((4, 2)),
+            dma((5, 2, 4)), dma((5, 2, 4)), dma((5, 2, 2)), dma((5, 2, 2)),
         ],
         compiler_params=pltpu.CompilerParams(
             collective_id=0, has_side_effects=True, vmem_limit_bytes=VMEM_LIMIT

time: 44.9 us -> 44.4 us (0.989)
  Pallas kernels: 44.8 us -> 44.3 us
    pallas_call x1, Pallas kernels: 39.7 us -> 39.2 us  [spectra_call(): pl.pallas_call(functools.partial(spectra_kernel, n_freq, n_pair), out_sha...]
where the time goes in v4:
time: 44.4 us; the launch traced here: 44.3 us
  Pallas kernels  44.3 us (100%)
    pallas_call x1, Pallas kernels, spectra_call(): pl.pallas_call(functools.partial(spectra_kernel, n_freq, n_pair), out_sha...  39.2 us
    pallas_call x1, Pallas kernels, correlate_call(): pl.pallas_call(functools.partial(correlate_kernel, n_freq, n_pair), out_s...  5.14 us

profile of v4, /device:TPU:1, one launch (start us, length us, event | category | flops | bytes accessed | tf_op | source)
XLA Modules:
  0.0 44.3 jit_solution(2670876309722684359)
XLA Ops:
  0.0 39.2 %shard_map.46 = (bf16[2,4,32,16,128]{4,3,2,1,0:T(8,128)(2,1)S(1)}, bf16[4,32,16,128]{3,2,1,0:T(8,128)(2,1)S(1)}, bf16[4,32,16,128]{3,2,1,0:T(8,128)(2,1)S(1)}, b...) custom-call(s32[103,16,2048]{2,1,0:T(8,128)} %bitcast.1, f32[8,2048]{1,0:T(8,128)} %constant.4.clone.taps_hbm, ...), custom_call_target="tpu_custom_call" | custom-call | tf_op jit(solution)/shard_map/pallas_call | solution.py:436
  39.2 5.1 %shard_map.47 = bf16[3,2,512,2048]{3,2,1,0:T(8,128)(2,1)} custom-call(bf16[2,4,32,16,128]{4,3,2,1,0:T(8,128)(2,1)S(1)} %get-tuple-element.10.x_ref, bf16[4,32,16,128]{3,2,1,0:T(8,128)(2,1)S(1)} %get-tuple-element.11.mid_ref, bf16[4,32,16,128]{3,2,1,0:T(8,128)(2,1)S(1)} %get-tuple-element.12.end_ref, bf16[4,16,16,128]{3,2,1,0:T(8,128)(2,1)S(1)} %get-tuple-element.13.x4_ref, ...), custom_call_target="tpu_custom_call" | custom-call | tf_op jit(solution)/shard_map/pallas_call | solution.py:517

commit v5 on v4

--- a/solution.py
+++ b/solution.py
@@ -376,14 +376,13 @@
     pl.when(early)(take(0, 0))
     rearrange(1)
     turn(1)
-    pl.when(early)(take(0, 1))
     pl.when(late)(lambda: forward(0, 0, 3))
 
     def between():
         forward(1, 0, 3)
         turn_and_spread(1, 0)
 
-    channelize(2, [(2, late, between), (3, late, take(1, 1)), (2, early, lambda: forward(0, 0, 3))])
+    channelize(2, [(2, late, between), (3, late, take(1, 1)), (1, early, take(0, 1)), (2, early, lambda: forward(0, 0, 3))])
 
     @pl.when(early)
     def _():
@@ -401,16 +400,14 @@
     spread(1, False, 2, 4)
     finish(row)
     rows_early()
-    keep(1).start()
-    keep(2).start()
-    keep(3).start()
     rows_late()
-    keep(4).start()
+    forward(0, 2, 4)
     arrived(0, 1, 3)
     finish(right)
-    forward(0, 2, 4)
     finish(left)
     forward(1, 2, 4)
+    for k in range(1, 5):
+        keep(k).start()
     passed(0, 1, 3)
     finish(lax.rem(row + 2, n_pair))
     arrived(2, 4)

time: 44.4 us -> 44 us (level)
  no operation moved by 1% of the time
where the time goes in v5:
time: 44 us; the launch traced here: 43.9 us
  Pallas kernels  43.9 us (100%)
    pallas_call x1, Pallas kernels, spectra_call(): pl.pallas_call(functools.partial(spectra_kernel, n_freq, n_pair), out_sha...  38.8 us
    pallas_call x1, Pallas kernels, correlate_call(): pl.pallas_call(functools.partial(correlate_kernel, n_freq, n_pair), out_s...  5.14 us

profile of v5, /device:TPU:1, one launch (start us, length us, event | category | flops | bytes accessed | tf_op | source)
XLA Modules:
  0.0 43.9 jit_solution(5314234422233539364)
XLA Ops:
  0.0 38.8 %shard_map.46 = (bf16[2,4,32,16,128]{4,3,2,1,0:T(8,128)(2,1)S(1)}, bf16[4,32,16,128]{3,2,1,0:T(8,128)(2,1)S(1)}, bf16[4,32,16,128]{3,2,1,0:T(8,128)(2,1)S(1)}, b...) custom-call(s32[103,16,2048]{2,1,0:T(8,128)} %bitcast.1, f32[8,2048]{1,0:T(8,128)} %constant.4.clone.taps_hbm, ...), custom_call_target="tpu_custom_call" | custom-call | tf_op jit(solution)/shard_map/pallas_call | solution.py:433
  38.8 5.1 %shard_map.47 = bf16[3,2,512,2048]{3,2,1,0:T(8,128)(2,1)} custom-call(bf16[2,4,32,16,128]{4,3,2,1,0:T(8,128)(2,1)S(1)} %get-tuple-element.10.x_ref, bf16[4,32,16,128]{3,2,1,0:T(8,128)(2,1)S(1)} %get-tuple-element.11.mid_ref, bf16[4,32,16,128]{3,2,1,0:T(8,128)(2,1)S(1)} %get-tuple-element.12.end_ref, bf16[4,16,16,128]{3,2,1,0:T(8,128)(2,1)S(1)} %get-tuple-element.13.x4_ref, ...), custom_call_target="tpu_custom_call" | custom-call | tf_op jit(solution)/shard_map/pallas_call | solution.py:514
